TPU v7x, 128 devices: a whole 4x4x4 slice. The times are simulated.
128 devices in a mesh: sec: 8 (over x, core), key: 16 (over y, z).
Axes of the slice: x: 4, y: 4, z: 4, core: 2. Of those that a mesh axis runs over, the one named last changes fastest.
Arguments:
- query: bfloat16 [16384, 16, 128], P(('sec', 'key')), may hold values from -64 to 64
- key: bfloat16 [16384, 4, 128], P(('sec', 'key')), may hold values from -5 to 5
- value: bfloat16 [16384, 4, 128], P(('sec', 'key')), may hold values from -5 to 5
- raw_directions: bfloat16 [16384, 4, 128], P(('sec', 'key')), may hold values from -5 to 5
- beta_raw_logits: float32 [16384, 4], P(('sec', 'key')), may hold values from -7 to 7
Outputs:
- attended: bfloat16 [16384, 16, 128], P(('sec', 'key'))
All inputs are finite; a program needn't handle non-finite values.
Results may differ from a plain program's by a relative error of at most 0.0055.
Values sent between devices are 32-bit elements; how exact they have to be, the bound alone decides.
A program may use at most 64 MiB of HBM per device.

v0:
```python
import math

import jax
import jax.numpy as jnp
from jax import lax
from jax.sharding import PartitionSpec as P

highest = lax.Precision.HIGHEST


def shifted(value, axis, steps):
    count = lax.axis_size(axis)
    first, last = (max(0, -steps), min(count, count - steps))
    return lax.ppermute(value, axis, [(source, source + steps) for source in range(first, last)])


def carried_in(value, axis, join, neutral, backward):
    count, mine = (lax.axis_size(axis), lax.axis_index(axis))
    pieces = lax.all_gather(value, axis)
    if backward:
        pieces = pieces[::-1]
        mine = count - 1 - mine
    total = jnp.full_like(value, 0) + jnp.asarray(neutral, value.dtype)

    def turn(position, total):
        longer = join(total, pieces[position])
        return jnp.where(position < mine, longer, total)

    return lax.fori_loop(0, count - 1, turn, total)


def block_terms(query, key, raw_directions, beta_raw_logits):
    length = key.shape[0]
    heads = key.shape[1]
    width = key.shape[2]
    query_group = query.shape[1] // heads
    w_float = raw_directions.astype(jnp.float32)
    w_unit = w_float / jnp.sqrt(jnp.sum(w_float * w_float, -1, keepdims=True) + 1e-06)
    beta = 2.0 * jax.nn.sigmoid(beta_raw_logits)
    w_heads = jnp.transpose(w_unit, (1, 0, 2))
    k_heads = jnp.transpose(key.astype(jnp.float32), (1, 0, 2))
    b_heads = jnp.transpose(beta, (1, 0))[:, :, None]
    positions = jnp.arange(length)
    strict = (positions[:, None] > positions[None, :]).astype(jnp.float32)
    lower = (positions[:, None] >= positions[None, :]).astype(jnp.float32)
    gram = jnp.einsum("hte,hse->hts", w_heads, w_heads, precision=highest) * strict
    system = jnp.eye(length, dtype=jnp.float32) + b_heads * gram
    cross = jnp.einsum("hte,hse->hts", w_heads, k_heads, precision=highest) * strict
    right = jnp.concatenate([b_heads * w_heads, b_heads * cross], axis=2)
    solved = lax.linalg.triangular_solve(
        system, right, left_side=True, lower=True, unit_diagonal=True
    )
    y_rows = solved[:, :, :width]
    z_rows = solved[:, :, width:]
    block_map = jnp.eye(width, dtype=jnp.float32) - jnp.einsum(
        "hte,htf->hef", w_heads, y_rows, precision=highest
    )
    key_end = k_heads - jnp.einsum("hts,hte->hse", z_rows, w_heads, precision=highest)
    q_heads = jnp.transpose(
        query.astype(jnp.float32).reshape(length, heads, query_group, width), (1, 2, 0, 3)
    )
    q_dot_w = jnp.einsum("hgie,hte->hgit", q_heads, w_heads, precision=highest) * lower
    query_start = q_heads - jnp.einsum("hgit,hte->hgie", q_dot_w, y_rows, precision=highest)
    inner = jnp.einsum("hgie,hje->hgij", q_heads, k_heads, precision=highest)
    inner = inner - jnp.einsum("hgit,htj->hgij", q_dot_w, z_rows, precision=highest)
    query_start = query_start.reshape(heads, query_group * length, width)
    inner = inner.reshape(heads, query_group * length, length) * width ** (-0.5)
    return (query_start, key_end, block_map, inner)


def attend(state, scores, values, valid):
    score_maxima, weighted_totals, exponent_sums = state
    masked = jnp.where(valid, scores, -1e30)
    new_max = jnp.maximum(score_maxima, jnp.max(masked, -1))
    weights = jnp.where(valid, jnp.exp(masked - new_max[..., None]), 0.0)
    factor = jnp.exp(score_maxima - new_max)
    weighted_totals = weighted_totals * factor + jnp.sum(weights, -1)
    rounded = weights.astype(jnp.bfloat16)
    exponent_sums = exponent_sums * factor[..., None] + jnp.einsum(
        "...ij,...je->...ie", rounded, values, preferred_element_type=jnp.float32
    )
    return (new_max, weighted_totals, exponent_sums)


def attend_packet(state, queries_flat, packet, valid, width):
    count = packet.shape[0]
    block = math.gcd(count, 512)
    scale_factor = width ** (-0.5)

    def one_block(index, carry):
        piece = lax.dynamic_slice_in_dim(packet, index * block, block, 0)
        scores = (
            jnp.einsum("ie,je->ij", queries_flat, piece[:, :width], precision=highest)
            * scale_factor
        )
        return attend(carry, scores, piece[:, width:].astype(jnp.bfloat16), valid)

    return lax.fori_loop(0, count // block, one_block, state)


def later_first(earlier, later):
    return jnp.einsum("hij,hjk->hik", later, earlier, precision=highest)


def earlier_first(earlier, later):
    return jnp.einsum("hij,hjk->hik", earlier, later, precision=highest)


def body(query, key, value, raw_directions, beta_raw_logits):
    length = query.shape[0]
    q_count = query.shape[1]
    width = query.shape[2]
    kv_heads = key.shape[1]
    query_group = q_count // kv_heads
    key_count = lax.axis_size("key")
    sec_count = lax.axis_size("sec")
    key_index = lax.axis_index("key")
    sec_index = lax.axis_index("sec")
    per_slot = q_count // key_count
    repeat_count = key_count // kv_heads
    rows_section = length * key_count
    scale_factor = width ** (-0.5)
    query_start, key_end, block_map, inner = block_terms(
        query, key, raw_directions, beta_raw_logits
    )
    value_head_rows = jnp.transpose(value, (1, 0, 2))
    positions = jnp.arange(length)
    causal = jnp.tile(positions[:, None] >= positions[None, :], (query_group, 1))
    local = (
        jnp.full((kv_heads, query_group * length), -1e30, jnp.float32),
        jnp.zeros((kv_heads, query_group * length), jnp.float32),
        jnp.zeros((kv_heads, query_group * length, width), jnp.float32),
    )
    local = attend(local, inner, value_head_rows, causal)
    packed = jnp.concatenate([key_end, value_head_rows.astype(jnp.float32)], axis=2)

    def relay_step(step, carry):
        outgoing = carry[0]
        arrived = shifted(outgoing, "key", 1)
        keys_in = arrived[:, :, :width]
        scores = jnp.einsum("hie,hje->hij", query_start, keys_in, precision=highest) * scale_factor
        state = attend(
            carry[1:], scores, arrived[:, :, width:].astype(jnp.bfloat16), key_index - step >= 0
        )
        moved = jnp.einsum("hje,hfe->hjf", keys_in, block_map, precision=highest)
        return (jnp.concatenate([moved, arrived[:, :, width:]], axis=2),) + state

    local = lax.fori_loop(1, key_count, relay_step, (packed,) + local)[1:]
    eye_maps = jnp.broadcast_to(jnp.eye(width, dtype=jnp.float32), block_map.shape)
    before = carried_in(block_map, "key", later_first, eye_maps, False)
    after = carried_in(block_map, "key", earlier_first, eye_maps, True)
    section_map = jnp.einsum(
        "hij,hjk->hik",
        after,
        jnp.einsum("hij,hjk->hik", block_map, before, precision=highest),
        precision=highest,
    )
    query_section = jnp.einsum("hie,hef->hif", query_start, before, precision=highest)
    query_section = jnp.transpose(
        query_section.reshape(kv_heads, query_group, length, width), (2, 0, 1, 3)
    )
    key_section = jnp.einsum("hje,hfe->hjf", key_end, after, precision=highest)
    key_pack = jnp.concatenate(
        [jnp.transpose(key_section, (1, 0, 2)), value.astype(jnp.float32)], axis=2
    )
    own_map = lax.dynamic_index_in_dim(section_map, key_index // repeat_count, 0, keepdims=False)
    query_slots = query_section.reshape(length, key_count, per_slot, width)
    key_slots = jnp.repeat(key_pack, repeat_count, axis=1)
    slot_queries, slot_keys = (
        lax.all_to_all(query_slots, "key", split_axis=1, concat_axis=0, tiled=True),
        lax.all_to_all(key_slots, "key", split_axis=1, concat_axis=0, tiled=True),
    )
    slot_flat = jnp.transpose(
        slot_queries.reshape(rows_section, per_slot, width), (1, 0, 2)
    ).reshape(per_slot * rows_section, width)
    slot_keys = slot_keys.reshape(rows_section, 2 * width)
    flat_rows = slot_flat.shape[0]
    distant = (
        jnp.full((flat_rows,), -1e30, jnp.float32),
        jnp.zeros((flat_rows,), jnp.float32),
        jnp.zeros((flat_rows, width), jnp.float32),
    )

    def walk_step(step, carry):
        arrived = shifted(carry[0], "sec", 1)
        state = attend_packet(carry[1:], slot_flat, arrived, sec_index - step >= 0, width)
        moved = jnp.einsum("je,fe->jf", arrived[:, :width], own_map, precision=highest)
        return (jnp.concatenate([moved, arrived[:, width:]], axis=1),) + state

    distant = lax.fori_loop(1, sec_count, walk_step, (slot_keys,) + distant)[1:]
    far_max = jnp.transpose(distant[0].reshape(per_slot, rows_section), (1, 0))
    far_total = jnp.transpose(distant[1].reshape(per_slot, rows_section), (1, 0))
    far_sums = jnp.transpose(distant[2].reshape(per_slot, rows_section, width), (1, 0, 2))
    back_sums, back_max, back_total = (
        lax.all_to_all(far_sums, "key", split_axis=0, concat_axis=1, tiled=True),
        lax.all_to_all(far_max, "key", split_axis=0, concat_axis=1, tiled=True),
        lax.all_to_all(far_total, "key", split_axis=0, concat_axis=1, tiled=True),
    )
    near_max = jnp.transpose(local[0].reshape(kv_heads, query_group, length), (2, 0, 1)).reshape(
        length, q_count
    )
    near_total = jnp.transpose(local[1].reshape(kv_heads, query_group, length), (2, 0, 1)).reshape(
        length, q_count
    )
    near_sums = jnp.transpose(
        local[2].reshape(kv_heads, query_group, length, width), (2, 0, 1, 3)
    ).reshape(length, q_count, width)
    joint_max = jnp.maximum(near_max, back_max)
    near_factor = jnp.exp(near_max - joint_max)
    far_factor = jnp.exp(back_max - joint_max)
    weighted_totals = near_total * near_factor + back_total * far_factor
    exponent_sums = near_sums * near_factor[..., None] + back_sums * far_factor[..., None]
    return (exponent_sums / weighted_totals[..., None]).astype(jnp.bfloat16)


def solution(mesh):
    return jax.shard_map(
        body,
        mesh=mesh,
        in_specs=(
            P(("sec", "key"), None, None),
            P(("sec", "key"), None, None),
            P(("sec", "key"), None, None),
            P(("sec", "key"), None, None),
            P(("sec", "key"), None),
        ),
        out_specs=P(("sec", "key"), None, None),
        check_vma=False,
    )
```

profile of v0, /device:TPU:26, one launch (start us, length us, event | category | flops | bytes accessed | tf_op | source)
XLA Modules:
  0.0 1158.6 jit_solution(8939084057140145272)
XLA Ops:
  11.3 39.3 %custom-call.3 = f32[4,1,128,128]{2,3,1,0:T(8,128)S(1)} custom-call(f32[4,1,128,128]{3,2,1,0:T(8,128)S(1)} %fusion.41), custom_call_target="InvertDiagBlocksLowerTriangular" | custom-call | tf_op jit(solution)/shard_map/triangular_solve | solution.py:50
  67.7 42.0 %all-gather.3.cloned.1.call-done = f32[64,128,128]{2,1,0:T(8,128)} async-done(((f32[4,128,128]{2,1,0:T(8,128)}), f32[64,128,128]{2,1,0:T(8,128)}) %all-gather.3.cloned.1.call-update) | async-done | bytes 4194320 | tf_op jit(solution)/shard_map/all_gather | solution.py:19
  114.4 24.3 %while.96 = (s32[]{:T(128)}, f32[4,128,128]{1,2,0:T(8,128)S(1)}, s32[]{:T(128)}, f32[16,4,128,128]{3,2,1,0:T(8,128)}, s32[]{:T(128)}) while((s32[]{:T(128)}, f32[4,128,128]{1,2,0:T(8,128)S(1)}, s32[]{:T(128)}, f32[16,4,128,128]{3,2,1,0:T(8,128)}, s32[]{:T(128)}) %tuple.162), condition=%wide.region_8.9_spmd, body=%wide.region_7.8_spmd.sunk | while | flops 100728832 | bytes 1573447 | solution.py:29
  146.7 21.1 %while.97 = (s32[]{:T(128)}, f32[4,128,128]{2,1,0:T(8,128)S(1)}, s32[]{:T(128)}, f32[16,4,128,128]{3,2,1,0:T(8,128)}, s32[]{:T(128)}) while((s32[]{:T(128)}, f32[4,128,128]{2,1,0:T(8,128)S(1)}, s32[]{:T(128)}, f32[16,4,128,128]{3,2,1,0:T(8,128)}, s32[]{:T(128)}) %tuple.179), condition=%wide.region_10.11_spmd, body=%wide.region_9.10_spmd.sunk | while | flops 100728832 | bytes 1573447 | solution.py:29
  196.1 643.7 %while.99 = (s32[]{:T(128)}, f32[2048,256]{0,1:T(8,128)}, f32[2048]{0:T(1024)}, f32[2048]{0:T(1024)}, f32[2048,128]{1,0:T(8,128)}, /*index=5*/f32[128,128]{1,0:T...) while((s32[]{:T(128)}, f32[2048,256]{0,1:T(8,128)}, ...), condition=%wide.region_16.17_spmd, body=%wide.region_11.16_spmd.sunk | while | flops 2296385536 | bytes 52494812 | solution.py:190
  198.1 25.7 %collective-permute-done.1 = f32[2048,256]{0,1:T(8,128)} collective-permute-done((f32[2048,256]{0,1:T(8,128)}, f32[2048,256]{0,1:T(8,128)}, u32[]{:S(2)}, u32[]{:S(2)}) %collective-permute-start.1) | collective-permute-done | bytes 2097184 | tf_op jit(solution)/shard_map/while/body/eval_jaxpr/ppermute | solution.py:14
  223.9 59.2 %while.100 = (s32[]{:T(128)}, f32[2048]{0:T(1024)}, f32[2048]{0:T(1024)}, f32[2048,128]{1,0:T(8,128)}, pred[]{:T(512)}, /*index=5*/f32[2048,256]{0,1:T(8,128)}, ...) while((s32[]{:T(128)}, f32[2048]{0:T(1024)}, f32[2048]{0:T(1024)}, ...), condition=%wide.region_15.15_spmd, body=%wide.region_12.14_spmd.sunk | while | flops 1893208064 | bytes 35651772 | solution.py:98
  290.1 25.7 %collective-permute-done.1 = f32[2048,256]{0,1:T(8,128)} collective-permute-done((f32[2048,256]{0,1:T(8,128)}, f32[2048,256]{0,1:T(8,128)}, u32[]{:S(2)}, u32[]{:S(2)}) %collective-permute-start.1) | collective-permute-done | bytes 2097184 | tf_op jit(solution)/shard_map/while/body/eval_jaxpr/ppermute | solution.py:14
  315.8 59.2 %while.100 = (s32[]{:T(128)}, f32[2048]{0:T(1024)}, f32[2048]{0:T(1024)}, f32[2048,128]{1,0:T(8,128)}, pred[]{:T(512)}, /*index=5*/f32[2048,256]{0,1:T(8,128)}, ...) while((s32[]{:T(128)}, f32[2048]{0:T(1024)}, f32[2048]{0:T(1024)}, ...), condition=%wide.region_15.15_spmd, body=%wide.region_12.14_spmd.sunk | while | flops 1893208064 | bytes 35651772 | solution.py:98
  382.0 25.7 %collective-permute-done.1 = f32[2048,256]{0,1:T(8,128)} collective-permute-done((f32[2048,256]{0,1:T(8,128)}, f32[2048,256]{0,1:T(8,128)}, u32[]{:S(2)}, u32[]{:S(2)}) %collective-permute-start.1) | collective-permute-done | bytes 2097184 | tf_op jit(solution)/shard_map/while/body/eval_jaxpr/ppermute | solution.py:14
  407.7 59.2 %while.100 = (s32[]{:T(128)}, f32[2048]{0:T(1024)}, f32[2048]{0:T(1024)}, f32[2048,128]{1,0:T(8,128)}, pred[]{:T(512)}, /*index=5*/f32[2048,256]{0,1:T(8,128)}, ...) while((s32[]{:T(128)}, f32[2048]{0:T(1024)}, f32[2048]{0:T(1024)}, ...), condition=%wide.region_15.15_spmd, body=%wide.region_12.14_spmd.sunk | while | flops 1893208064 | bytes 35651772 | solution.py:98
  474.0 25.7 %collective-permute-done.1 = f32[2048,256]{0,1:T(8,128)} collective-permute-done((f32[2048,256]{0,1:T(8,128)}, f32[2048,256]{0,1:T(8,128)}, u32[]{:S(2)}, u32[]{:S(2)}) %collective-permute-start.1) | collective-permute-done | bytes 2097184 | tf_op jit(solution)/shard_map/while/body/eval_jaxpr/ppermute | solution.py:14
  499.7 59.2 %while.100 = (s32[]{:T(128)}, f32[2048]{0:T(1024)}, f32[2048]{0:T(1024)}, f32[2048,128]{1,0:T(8,128)}, pred[]{:T(512)}, /*index=5*/f32[2048,256]{0,1:T(8,128)}, ...) while((s32[]{:T(128)}, f32[2048]{0:T(1024)}, f32[2048]{0:T(1024)}, ...), condition=%wide.region_15.15_spmd, body=%wide.region_12.14_spmd.sunk | while | flops 1893208064 | bytes 35651772 | solution.py:98
  565.9 25.7 %collective-permute-done.1 = f32[2048,256]{0,1:T(8,128)} collective-permute-done((f32[2048,256]{0,1:T(8,128)}, f32[2048,256]{0,1:T(8,128)}, u32[]{:S(2)}, u32[]{:S(2)}) %collective-permute-start.1) | collective-permute-done | bytes 2097184 | tf_op jit(solution)/shard_map/while/body/eval_jaxpr/ppermute | solution.py:14
  591.6 59.2 %while.100 = (s32[]{:T(128)}, f32[2048]{0:T(1024)}, f32[2048]{0:T(1024)}, f32[2048,128]{1,0:T(8,128)}, pred[]{:T(512)}, /*index=5*/f32[2048,256]{0,1:T(8,128)}, ...) while((s32[]{:T(128)}, f32[2048]{0:T(1024)}, f32[2048]{0:T(1024)}, ...), condition=%wide.region_15.15_spmd, body=%wide.region_12.14_spmd.sunk | while | flops 1893208064 | bytes 35651772 | solution.py:98
  657.8 25.7 %collective-permute-done.1 = f32[2048,256]{0,1:T(8,128)} collective-permute-done((f32[2048,256]{0,1:T(8,128)}, f32[2048,256]{0,1:T(8,128)}, u32[]{:S(2)}, u32[]{:S(2)}) %collective-permute-start.1) | collective-permute-done | bytes 2097184 | tf_op jit(solution)/shard_map/while/body/eval_jaxpr/ppermute | solution.py:14
  683.6 59.2 %while.100 = (s32[]{:T(128)}, f32[2048]{0:T(1024)}, f32[2048]{0:T(1024)}, f32[2048,128]{1,0:T(8,128)}, pred[]{:T(512)}, /*index=5*/f32[2048,256]{0,1:T(8,128)}, ...) while((s32[]{:T(128)}, f32[2048]{0:T(1024)}, f32[2048]{0:T(1024)}, ...), condition=%wide.region_15.15_spmd, body=%wide.region_12.14_spmd.sunk | while | flops 1893208064 | bytes 35651772 | solution.py:98
  749.8 25.7 %collective-permute-done.1 = f32[2048,256]{0,1:T(8,128)} collective-permute-done((f32[2048,256]{0,1:T(8,128)}, f32[2048,256]{0,1:T(8,128)}, u32[]{:S(2)}, u32[]{:S(2)}) %collective-permute-start.1) | collective-permute-done | bytes 2097184 | tf_op jit(solution)/shard_map/while/body/eval_jaxpr/ppermute | solution.py:14
  775.5 59.2 %while.100 = (s32[]{:T(128)}, f32[2048]{0:T(1024)}, f32[2048]{0:T(1024)}, f32[2048,128]{1,0:T(8,128)}, pred[]{:T(512)}, /*index=5*/f32[2048,256]{0,1:T(8,128)}, ...) while((s32[]{:T(128)}, f32[2048]{0:T(1024)}, f32[2048]{0:T(1024)}, ...), condition=%wide.region_15.15_spmd, body=%wide.region_12.14_spmd.sunk | while | flops 1893208064 | bytes 35651772 | solution.py:98
  868.2 280.4 %while.95 = (s32[]{:T(128)}, f32[4,128,256]{2,1,0:T(8,128)S(1)}, f32[4,512]{1,0:T(4,128)S(1)}, f32[4,512]{1,0:T(4,128)S(1)}, f32[4,512,128]{2,1,0:T(8,128)S(1)},...) while((s32[]{:T(128)}, f32[4,128,256]{2,1,0:T(8,128)S(1)}, ...), condition=%wide.region_6.7_spmd, body=%wide.region_3.6_spmd.sunk | while | flops 573444096 | bytes 11272357 | solution.py:148
  871.6 21.0 %collective-permute-done = f32[4,128,256]{2,1,0:T(8,128)S(1)} collective-permute-done((f32[4,128,256]{2,1,0:T(8,128)S(1)}, f32[4,128,256]{2,1,0:T(8,128)S(1)}, u32[]{:S(2)}, u32[]{:S(2)}) %collective-permute-start) | collective-permute-done | bytes 524320 | tf_op jit(solution)/shard_map/while/body/eval_jaxpr/ppermute | solution.py:14
  897.3 11.8 %collective-permute-done = f32[4,128,256]{2,1,0:T(8,128)S(1)} collective-permute-done((f32[4,128,256]{2,1,0:T(8,128)S(1)}, f32[4,128,256]{2,1,0:T(8,128)S(1)}, u32[]{:S(2)}, u32[]{:S(2)}) %collective-permute-start) | collective-permute-done | bytes 524320 | tf_op jit(solution)/shard_map/while/body/eval_jaxpr/ppermute | solution.py:14
  929.9 11.2 collective-permute-done
  961.9 11.4 collective-permute-done
  978.0 12.4 %collective-permute-done = f32[4,128,256]{2,1,0:T(8,128)S(1)} collective-permute-done((f32[4,128,256]{2,1,0:T(8,128)S(1)}, f32[4,128,256]{2,1,0:T(8,128)S(1)}, u32[]{:S(2)}, u32[]{:S(2)}) %collective-permute-start) | collective-permute-done | bytes 524320 | tf_op jit(solution)/shard_map/while/body/eval_jaxpr/ppermute | solution.py:14
  995.2 13.5 %collective-permute-done = f32[4,128,256]{2,1,0:T(8,128)S(1)} collective-permute-done((f32[4,128,256]{2,1,0:T(8,128)S(1)}, f32[4,128,256]{2,1,0:T(8,128)S(1)}, u32[]{:S(2)}, u32[]{:S(2)}) %collective-permute-start) | collective-permute-done | bytes 524320 | tf_op jit(solution)/shard_map/while/body/eval_jaxpr/ppermute | solution.py:14
  1013.5 14.6 %collective-permute-done = f32[4,128,256]{2,1,0:T(8,128)S(1)} collective-permute-done((f32[4,128,256]{2,1,0:T(8,128)S(1)}, f32[4,128,256]{2,1,0:T(8,128)S(1)}, u32[]{:S(2)}, u32[]{:S(2)}) %collective-permute-start) | collective-permute-done | bytes 524320 | tf_op jit(solution)/shard_map/while/body/eval_jaxpr/ppermute | solution.py:14
  1032.8 15.7 %collective-permute-done = f32[4,128,256]{2,1,0:T(8,128)S(1)} collective-permute-done((f32[4,128,256]{2,1,0:T(8,128)S(1)}, f32[4,128,256]{2,1,0:T(8,128)S(1)}, u32[]{:S(2)}, u32[]{:S(2)}) %collective-permute-start) | collective-permute-done | bytes 524320 | tf_op jit(solution)/shard_map/while/body/eval_jaxpr/ppermute | solution.py:14
  1053.3 16.8 %collective-permute-done = f32[4,128,256]{2,1,0:T(8,128)S(1)} collective-permute-done((f32[4,128,256]{2,1,0:T(8,128)S(1)}, f32[4,128,256]{2,1,0:T(8,128)S(1)}, u32[]{:S(2)}, u32[]{:S(2)}) %collective-permute-start) | collective-permute-done | bytes 524320 | tf_op jit(solution)/shard_map/while/body/eval_jaxpr/ppermute | solution.py:14
  1074.9 16.0 %collective-permute-done = f32[4,128,256]{2,1,0:T(8,128)S(1)} collective-permute-done((f32[4,128,256]{2,1,0:T(8,128)S(1)}, f32[4,128,256]{2,1,0:T(8,128)S(1)}, u32[]{:S(2)}, u32[]{:S(2)}) %collective-permute-start) | collective-permute-done | bytes 524320 | tf_op jit(solution)/shard_map/while/body/eval_jaxpr/ppermute | solution.py:14
  1095.6 15.1 %collective-permute-done = f32[4,128,256]{2,1,0:T(8,128)S(1)} collective-permute-done((f32[4,128,256]{2,1,0:T(8,128)S(1)}, f32[4,128,256]{2,1,0:T(8,128)S(1)}, u32[]{:S(2)}, u32[]{:S(2)}) %collective-permute-start) | collective-permute-done | bytes 524320 | tf_op jit(solution)/shard_map/while/body/eval_jaxpr/ppermute | solution.py:14
  1115.5 14.2 %collective-permute-done = f32[4,128,256]{2,1,0:T(8,128)S(1)} collective-permute-done((f32[4,128,256]{2,1,0:T(8,128)S(1)}, f32[4,128,256]{2,1,0:T(8,128)S(1)}, u32[]{:S(2)}, u32[]{:S(2)}) %collective-permute-start) | collective-permute-done | bytes 524320 | tf_op jit(solution)/shard_map/while/body/eval_jaxpr/ppermute | solution.py:14
  (711 shorter events, 705.6 us)
Async XLA Ops:
  6.5 103.1 %all-gather.3.cloned.1.call-start = ((), (), s32[]{:S(2)}) async-start(), calls=%async_computation.5 | async-start | bytes 4456448 | tf_op jit(solution)/shard_map/all_gather | solution.py:19
  141.0 33.5 %all-to-all-start = ((f32[128,16,256]{0,2,1:T(8,128)}), f32[128,16,256]{0,2,1:T(8,128)}, u32[]{:S(2)}, u32[]{:S(2)}) async-start(f32[128,16,256]{0,2,1:T(8,128)} %bitcast.199), calls=%async_computation | async-start | bytes 4194304 | tf_op jit(solution)/shard_map/all_to_all | solution.py:171
  174.5 19.4 %all-to-all-start.1 = ((f32[128,16,1,128]{3,0,2,1:T(8,128)}), f32[128,16,1,128]{3,0,2,1:T(8,128)S(1)}, u32[]{:S(2)}, u32[]{:S(2)}) async-start(f32[128,16,1,128]{3,0,2,1:T(8,128)} %bitcast.206), calls=%async_computation.1 | async-start | bytes 2097152 | tf_op jit(solution)/shard_map/all_to_all | solution.py:170
  196.0 649.4 %copy-start.6 = (bf16[4,512,128]{2,1,0:T(8,128)(2,1)S(1)}, bf16[4,512,128]{2,1,0:T(8,128)(2,1)}, u32[]{:S(2)}) copy-start(bf16[4,512,128]{2,1,0:T(8,128)(2,1)} %fusion.45) | copy-start | bytes 1572868
  196.0 649.4 %copy-start.12 = (bf16[128,4,128]{0,2,1:T(8,128)(2,1)S(1)}, bf16[128,4,128]{0,2,1:T(8,128)(2,1)}, u32[]{:S(2)}) copy-start(bf16[128,4,128]{0,2,1:T(8,128)(2,1)} %copy-done.11) | copy-start | bytes 393220
  196.0 649.4 %copy-start.21 = (f32[4,512]{1,0:T(4,128)S(1)}, f32[4,512]{1,0:T(4,128)}, u32[]{:S(2)}) copy-start(f32[4,512]{1,0:T(4,128)} %get-tuple-element.762) | copy-start | bytes 24580
  196.0 660.3 %copy-start.14 = (f32[4,128,128]{1,2,0:T(8,128)S(1)}, f32[4,128,128]{1,2,0:T(8,128)}, u32[]{:S(2)}) copy-start(f32[4,128,128]{1,2,0:T(8,128)} %convolution_subtract_fusion.3) | copy-start | bytes 786436
  196.1 27.8 %collective-permute-start.1 = (f32[2048,256]{0,1:T(8,128)}, f32[2048,256]{0,1:T(8,128)}, u32[]{:S(2)}, u32[]{:S(2)}) collective-permute-start(f32[2048,256]{0,1:T(8,128)} %get-tuple-element.1080), channel_id=1, source_target_pairs={{0,16},{16,32},{32,48},{48,64},{64,80},{80,96},{96,112},{1,17},{17... | collective-permute-start | bytes 6291464 | tf_op jit(solution)/shard_map/while/body/eval_jaxpr/ppermute | solution.py:14
  288.1 27.7 %collective-permute-start.1 = (f32[2048,256]{0,1:T(8,128)}, f32[2048,256]{0,1:T(8,128)}, u32[]{:S(2)}, u32[]{:S(2)}) collective-permute-start(f32[2048,256]{0,1:T(8,128)} %get-tuple-element.1080), channel_id=1, source_target_pairs={{0,16},{16,32},{32,48},{48,64},{64,80},{80,96},{96,112},{1,17},{17... | collective-permute-start | bytes 6291464 | tf_op jit(solution)/shard_map/while/body/eval_jaxpr/ppermute | solution.py:14
  380.1 27.7 %collective-permute-start.1 = (f32[2048,256]{0,1:T(8,128)}, f32[2048,256]{0,1:T(8,128)}, u32[]{:S(2)}, u32[]{:S(2)}) collective-permute-start(f32[2048,256]{0,1:T(8,128)} %get-tuple-element.1080), channel_id=1, source_target_pairs={{0,16},{16,32},{32,48},{48,64},{64,80},{80,96},{96,112},{1,17},{17... | collective-permute-start | bytes 6291464 | tf_op jit(solution)/shard_map/while/body/eval_jaxpr/ppermute | solution.py:14
  472.0 27.7 %collective-permute-start.1 = (f32[2048,256]{0,1:T(8,128)}, f32[2048,256]{0,1:T(8,128)}, u32[]{:S(2)}, u32[]{:S(2)}) collective-permute-start(f32[2048,256]{0,1:T(8,128)} %get-tuple-element.1080), channel_id=1, source_target_pairs={{0,16},{16,32},{32,48},{48,64},{64,80},{80,96},{96,112},{1,17},{17... | collective-permute-start | bytes 6291464 | tf_op jit(solution)/shard_map/while/body/eval_jaxpr/ppermute | solution.py:14
  564.0 27.7 %collective-permute-start.1 = (f32[2048,256]{0,1:T(8,128)}, f32[2048,256]{0,1:T(8,128)}, u32[]{:S(2)}, u32[]{:S(2)}) collective-permute-start(f32[2048,256]{0,1:T(8,128)} %get-tuple-element.1080), channel_id=1, source_target_pairs={{0,16},{16,32},{32,48},{48,64},{64,80},{80,96},{96,112},{1,17},{17... | collective-permute-start | bytes 6291464 | tf_op jit(solution)/shard_map/while/body/eval_jaxpr/ppermute | solution.py:14
  655.9 27.7 %collective-permute-start.1 = (f32[2048,256]{0,1:T(8,128)}, f32[2048,256]{0,1:T(8,128)}, u32[]{:S(2)}, u32[]{:S(2)}) collective-permute-start(f32[2048,256]{0,1:T(8,128)} %get-tuple-element.1080), channel_id=1, source_target_pairs={{0,16},{16,32},{32,48},{48,64},{64,80},{80,96},{96,112},{1,17},{17... | collective-permute-start | bytes 6291464 | tf_op jit(solution)/shard_map/while/body/eval_jaxpr/ppermute | solution.py:14
  747.9 27.7 %collective-permute-start.1 = (f32[2048,256]{0,1:T(8,128)}, f32[2048,256]{0,1:T(8,128)}, u32[]{:S(2)}, u32[]{:S(2)}) collective-permute-start(f32[2048,256]{0,1:T(8,128)} %get-tuple-element.1080), channel_id=1, source_target_pairs={{0,16},{16,32},{32,48},{48,64},{64,80},{80,96},{96,112},{1,17},{17... | collective-permute-start | bytes 6291464 | tf_op jit(solution)/shard_map/while/body/eval_jaxpr/ppermute | solution.py:14
  839.8 11.0 all-to-all-start.2
  850.8 10.9 all-to-all-start.4
  861.7 286.9 %all-to-all-start.3 = ((f32[2048,1,128]{2,1,0:T(1,128)}), f32[2048,1,128]{2,1,0:T(1,128)}, u32[]{:S(2)}, u32[]{:S(2)}) async-start(f32[2048,1,128]{2,1,0:T(1,128)} %bitcast.52), calls=%async_computation.3 | async-start | bytes 2097152 | tf_op jit(solution)/shard_map/all_to_all | solution.py:195
  868.2 24.4 %collective-permute-start = (f32[4,128,256]{2,1,0:T(8,128)S(1)}, f32[4,128,256]{2,1,0:T(8,128)S(1)}, u32[]{:S(2)}, u32[]{:S(2)}) collective-permute-start(f32[4,128,256]{2,1,0:T(8,128)S(1)} %get-tuple-element.1118), channel_id=1, source_target_pairs={{0,1},{1,2},{2,3},{3,4},{4,5},{5,6},{6,7},{7,8},{8,9},{9,10},{10,1... | collective-permute-start | bytes 1572872 | tf_op jit(solution)/shard_map/while/body/eval_jaxpr/ppermute | solution.py:14
  895.4 13.7 %collective-permute-start = (f32[4,128,256]{2,1,0:T(8,128)S(1)}, f32[4,128,256]{2,1,0:T(8,128)S(1)}, u32[]{:S(2)}, u32[]{:S(2)}) collective-permute-start(f32[4,128,256]{2,1,0:T(8,128)S(1)} %get-tuple-element.1118), channel_id=1, source_target_pairs={{0,1},{1,2},{2,3},{3,4},{4,5},{5,6},{6,7},{7,8},{8,9},{9,10},{10,1... | collective-permute-start | bytes 1572872 | tf_op jit(solution)/shard_map/while/body/eval_jaxpr/ppermute | solution.py:14
  911.9 13.2 %collective-permute-start = (f32[4,128,256]{2,1,0:T(8,128)S(1)}, f32[4,128,256]{2,1,0:T(8,128)S(1)}, u32[]{:S(2)}, u32[]{:S(2)}) collective-permute-start(f32[4,128,256]{2,1,0:T(8,128)S(1)} %get-tuple-element.1118), channel_id=1, source_target_pairs={{0,1},{1,2},{2,3},{3,4},{4,5},{5,6},{6,7},{7,8},{8,9},{9,10},{10,1... | collective-permute-start | bytes 1572872 | tf_op jit(solution)/shard_map/while/body/eval_jaxpr/ppermute | solution.py:14
  927.9 13.2 %collective-permute-start = (f32[4,128,256]{2,1,0:T(8,128)S(1)}, f32[4,128,256]{2,1,0:T(8,128)S(1)}, u32[]{:S(2)}, u32[]{:S(2)}) collective-permute-start(f32[4,128,256]{2,1,0:T(8,128)S(1)} %get-tuple-element.1118), channel_id=1, source_target_pairs={{0,1},{1,2},{2,3},{3,4},{4,5},{5,6},{6,7},{7,8},{8,9},{9,10},{10,1... | collective-permute-start | bytes 1572872 | tf_op jit(solution)/shard_map/while/body/eval_jaxpr/ppermute | solution.py:14
  943.9 13.2 %collective-permute-start = (f32[4,128,256]{2,1,0:T(8,128)S(1)}, f32[4,128,256]{2,1,0:T(8,128)S(1)}, u32[]{:S(2)}, u32[]{:S(2)}) collective-permute-start(f32[4,128,256]{2,1,0:T(8,128)S(1)} %get-tuple-element.1118), channel_id=1, source_target_pairs={{0,1},{1,2},{2,3},{3,4},{4,5},{5,6},{6,7},{7,8},{8,9},{9,10},{10,1... | collective-permute-start | bytes 1572872 | tf_op jit(solution)/shard_map/while/body/eval_jaxpr/ppermute | solution.py:14
  959.9 13.3 %collective-permute-start = (f32[4,128,256]{2,1,0:T(8,128)S(1)}, f32[4,128,256]{2,1,0:T(8,128)S(1)}, u32[]{:S(2)}, u32[]{:S(2)}) collective-permute-start(f32[4,128,256]{2,1,0:T(8,128)S(1)} %get-tuple-element.1118), channel_id=1, source_target_pairs={{0,1},{1,2},{2,3},{3,4},{4,5},{5,6},{6,7},{7,8},{8,9},{9,10},{10,1... | collective-permute-start | bytes 1572872 | tf_op jit(solution)/shard_map/while/body/eval_jaxpr/ppermute | solution.py:14
  976.0 14.4 %collective-permute-start = (f32[4,128,256]{2,1,0:T(8,128)S(1)}, f32[4,128,256]{2,1,0:T(8,128)S(1)}, u32[]{:S(2)}, u32[]{:S(2)}) collective-permute-start(f32[4,128,256]{2,1,0:T(8,128)S(1)} %get-tuple-element.1118), channel_id=1, source_target_pairs={{0,1},{1,2},{2,3},{3,4},{4,5},{5,6},{6,7},{7,8},{8,9},{9,10},{10,1... | collective-permute-start | bytes 1572872 | tf_op jit(solution)/shard_map/while/body/eval_jaxpr/ppermute | solution.py:14
  993.2 15.5 %collective-permute-start = (f32[4,128,256]{2,1,0:T(8,128)S(1)}, f32[4,128,256]{2,1,0:T(8,128)S(1)}, u32[]{:S(2)}, u32[]{:S(2)}) collective-permute-start(f32[4,128,256]{2,1,0:T(8,128)S(1)} %get-tuple-element.1118), channel_id=1, source_target_pairs={{0,1},{1,2},{2,3},{3,4},{4,5},{5,6},{6,7},{7,8},{8,9},{9,10},{10,1... | collective-permute-start | bytes 1572872 | tf_op jit(solution)/shard_map/while/body/eval_jaxpr/ppermute | solution.py:14
  1011.5 16.5 %collective-permute-start = (f32[4,128,256]{2,1,0:T(8,128)S(1)}, f32[4,128,256]{2,1,0:T(8,128)S(1)}, u32[]{:S(2)}, u32[]{:S(2)}) collective-permute-start(f32[4,128,256]{2,1,0:T(8,128)S(1)} %get-tuple-element.1118), channel_id=1, source_target_pairs={{0,1},{1,2},{2,3},{3,4},{4,5},{5,6},{6,7},{7,8},{8,9},{9,10},{10,1... | collective-permute-start | bytes 1572872 | tf_op jit(solution)/shard_map/while/body/eval_jaxpr/ppermute | solution.py:14
  1030.9 17.7 %collective-permute-start = (f32[4,128,256]{2,1,0:T(8,128)S(1)}, f32[4,128,256]{2,1,0:T(8,128)S(1)}, u32[]{:S(2)}, u32[]{:S(2)}) collective-permute-start(f32[4,128,256]{2,1,0:T(8,128)S(1)} %get-tuple-element.1118), channel_id=1, source_target_pairs={{0,1},{1,2},{2,3},{3,4},{4,5},{5,6},{6,7},{7,8},{8,9},{9,10},{10,1... | collective-permute-start | bytes 1572872 | tf_op jit(solution)/shard_map/while/body/eval_jaxpr/ppermute | solution.py:14
  1051.4 18.8 %collective-permute-start = (f32[4,128,256]{2,1,0:T(8,128)S(1)}, f32[4,128,256]{2,1,0:T(8,128)S(1)}, u32[]{:S(2)}, u32[]{:S(2)}) collective-permute-start(f32[4,128,256]{2,1,0:T(8,128)S(1)} %get-tuple-element.1118), channel_id=1, source_target_pairs={{0,1},{1,2},{2,3},{3,4},{4,5},{5,6},{6,7},{7,8},{8,9},{9,10},{10,1... | collective-permute-start | bytes 1572872 | tf_op jit(solution)/shard_map/while/body/eval_jaxpr/ppermute | solution.py:14
  1073.0 17.9 %collective-permute-start = (f32[4,128,256]{2,1,0:T(8,128)S(1)}, f32[4,128,256]{2,1,0:T(8,128)S(1)}, u32[]{:S(2)}, u32[]{:S(2)}) collective-permute-start(f32[4,128,256]{2,1,0:T(8,128)S(1)} %get-tuple-element.1118), channel_id=1, source_target_pairs={{0,1},{1,2},{2,3},{3,4},{4,5},{5,6},{6,7},{7,8},{8,9},{9,10},{10,1... | collective-permute-start | bytes 1572872 | tf_op jit(solution)/shard_map/while/body/eval_jaxpr/ppermute | solution.py:14
  1093.7 17.1 %collective-permute-start = (f32[4,128,256]{2,1,0:T(8,128)S(1)}, f32[4,128,256]{2,1,0:T(8,128)S(1)}, u32[]{:S(2)}, u32[]{:S(2)}) collective-permute-start(f32[4,128,256]{2,1,0:T(8,128)S(1)} %get-tuple-element.1118), channel_id=1, source_target_pairs={{0,1},{1,2},{2,3},{3,4},{4,5},{5,6},{6,7},{7,8},{8,9},{9,10},{10,1... | collective-permute-start | bytes 1572872 | tf_op jit(solution)/shard_map/while/body/eval_jaxpr/ppermute | solution.py:14
  1113.6 16.2 %collective-permute-start = (f32[4,128,256]{2,1,0:T(8,128)S(1)}, f32[4,128,256]{2,1,0:T(8,128)S(1)}, u32[]{:S(2)}, u32[]{:S(2)}) collective-permute-start(f32[4,128,256]{2,1,0:T(8,128)S(1)} %get-tuple-element.1118), channel_id=1, source_target_pairs={{0,1},{1,2},{2,3},{3,4},{4,5},{5,6},{6,7},{7,8},{8,9},{9,10},{10,1... | collective-permute-start | bytes 1572872 | tf_op jit(solution)/shard_map/while/body/eval_jaxpr/ppermute | solution.py:14
  1132.6 13.2 %collective-permute-start = (f32[4,128,256]{2,1,0:T(8,128)S(1)}, f32[4,128,256]{2,1,0:T(8,128)S(1)}, u32[]{:S(2)}, u32[]{:S(2)}) collective-permute-start(f32[4,128,256]{2,1,0:T(8,128)S(1)} %get-tuple-element.1118), channel_id=1, source_target_pairs={{0,1},{1,2},{2,3},{3,4},{4,5},{5,6},{6,7},{7,8},{8,9},{9,10},{10,1... | collective-permute-start | bytes 1572872 | tf_op jit(solution)/shard_map/while/body/eval_jaxpr/ppermute | solution.py:14
  (45 other events, 629.4 us)
Sparse Core Ops, SparseCore 0:
  55.8 53.7 all-gather.2
where the time goes:
time: 1170 us; the launch traced here: 1160 us
  waiting for transfers between devices  450 us (38%)
  matrix products  353 us (30%)
  other arithmetic  148 us (13%)
  local copies, waits for them, and re-layouts  116 us (10%)
  starting transfers between devices  73.3 us (6%)
  between operations  13.9 us (1%)
    ppermute x22, waiting for transfers between devices, shifted(): lax.ppermute(value, axis, [(source, source + steps) for source in range(f...  388 us
    dot_general x44, matrix products, attend(): jnp.einsum('...ij,...je->...ie', rounded, values, preferred_element_type=...  144 us
    dot_general x28, matrix products, one_block(): jnp.einsum('ie,je->ij', queries_flat, piece[:, :width], precision=highest)  106 us
    while x185, local copies, waits for them, and re-layouts  58.3 us
    ppermute x22, starting transfers between devices, shifted(): lax.ppermute(value, axis, [(source, source + steps) for source in range(f...  43.8 us
    all_gather x1, waiting for transfers between devices, carried_in(): pieces = lax.all_gather(value, axis)  42 us
    another operation x3, other arithmetic, block_terms(): lax.linalg.triangular_solve(system, right, left_side=True, lower=True, un...  39.4 us
    add x43, other arithmetic, attend(): weighted_totals = weighted_totals * factor + jnp.sum(weights, -1)  37.6 us
  transfers between devices with their start and end apart: 28, of which 27 were waited for; matrix products, arithmetic and copies ran while one was open for 7% of the time, Pallas kernels for 0%

commit v1 on v0

v1 whole, which is shorter than its diff:
```python
import functools
import math

import jax
import jax.numpy as jnp
from jax import lax
from jax.experimental import pallas as pl
from jax.experimental.pallas import tpu as pltpu
from jax.sharding import PartitionSpec as P

F32 = jnp.float32
BF16 = jnp.bfloat16
NN = ((1,), (0,))
NT = ((1,), (1,))
TN = ((0,), (0,))
LOW = -1e30
VMEM_LIMIT = 56 * 1024 * 1024
WIDE = 8


def halves(x):
    high = x.astype(BF16)
    return high, (x - high.astype(F32)).astype(BF16)


def left(x, axis):
    high, low = halves(x)
    return jnp.concatenate([high, low, high, low], axis)


def right(x, axis):
    high, low = halves(x)
    return jnp.concatenate([high, high, low, low], axis)


def mm(a, b, dims):
    return lax.dot_general(a, b, (dims, ((), ())), preferred_element_type=F32)


def fine(a, b, dims):
    return mm(left(a, dims[0][0]), right(b, dims[1][0]), dims)


def grids(n):
    return lax.broadcasted_iota(jnp.int32, (n, n), 0), lax.broadcasted_iota(jnp.int32, (n, n), 1)


def as_row(column, eye):
    return jnp.sum(jnp.where(eye, column, 0.0), 0, keepdims=True)


def as_column(row, eye):
    return jnp.sum(jnp.where(eye, row, 0.0), 1, keepdims=True)


def terms_kernel(scale, q_ref, k_ref, v_ref, w_ref, b_ref, x_ref, z_ref, qw_ref):
    heads, n, width = k_ref.shape
    group = q_ref.shape[0] // heads
    row, col = grids(n)
    units, betas, lows, inverses = [], [], [], []
    for h in range(heads):
        w = w_ref[h].astype(F32)
        unit = w / jnp.sqrt(jnp.sum(w * w, -1, keepdims=True) + 1e-6)
        beta = 2.0 / (1.0 + jnp.exp(-b_ref[:, h : h + 1]))
        low = jnp.where(row > col, beta * fine(unit, unit, NT), 0.0)
        first = ((row ^ col) == 1) & (row > col)
        units.append(unit)
        betas.append(beta)
        lows.append(low)
        inverses.append(jnp.where(row == col, 1.0, jnp.where(first, -low, 0.0)))
    size = 2
    while size < n:
        pick = ((row ^ col) < 2 * size) & ((row & size) != 0) & ((col & size) == 0)
        inner = [fine(jnp.where(pick, lows[h], 0.0), inverses[h], NN) for h in range(heads)]
        inverses = [inverses[h] - fine(inverses[h], inner[h], NN) for h in range(heads)]
        size *= 2
    for h in range(heads):
        unit, beta, inverse = units[h], betas[h], inverses[h]
        key = k_ref[h]
        high, low = halves(unit)
        both = jnp.concatenate([high, low], 1)
        cross = jnp.where(row > col, mm(both, jnp.concatenate([key, key], 1), NT), 0.0)
        solved = fine(inverse, jnp.concatenate([beta * unit, beta * cross], 1), NN)
        y, z = solved[:, :width], solved[:, width:]
        z_ref[h] = z
        block_map = jnp.where(row == col, 1.0, 0.0) - fine(unit, y, TN)
        key_end = key.astype(F32) - fine(z, unit, TN)
        value = v_ref[h].astype(F32)
        y_right = right(y, 0)
        for g in range(h * group, h * group + group):
            query = q_ref[g]
            qw = jnp.where(row >= col, mm(jnp.concatenate([query, query], 1), both, NT), 0.0)
            qw_ref[g] = qw
            x_ref[g, 0] = (query.astype(F32) - mm(left(qw, 1), y_right, NN)) * scale
            x_ref[g, 1] = key_end
            x_ref[g, 2] = value
            x_ref[g, 3] = block_map


def diagonal_kernel(scale, q_ref, k_ref, v_ref, z_ref, qw_ref, o_ref, m_ref, l_ref):
    heads, n, width = k_ref.shape
    group = q_ref.shape[0] // heads
    row, col = grids(n)
    for h in range(heads):
        z_right = right(z_ref[h], 0)
        for g in range(h * group, h * group + group):
            score = mm(q_ref[g], k_ref[h], NT) - mm(left(qw_ref[g], 1), z_right, NN)
            score = jnp.where(row >= col, score * scale, LOW)
            top = jnp.max(score, -1, keepdims=True)
            weight = jnp.exp2(score - top)
            m_ref[g] = top
            l_ref[g] = jnp.sum(weight, -1, keepdims=True)
            o_ref[g] = mm(weight.astype(BF16), v_ref[h], NN)


def frames_kernel(x_ref, q_ref, kv_ref, s_ref):
    blocks, _, n, width = x_ref.shape
    before, after = None, None
    for a in range(blocks):
        b = blocks - 1 - a
        query, key = x_ref[a, 0], x_ref[b, 1]
        kv_ref[b * n : b * n + n, width:] = x_ref[b, 2]
        if a == 0:
            q_ref[:n] = query
            kv_ref[b * n : b * n + n, :width] = key
            before, after = x_ref[a, 3], x_ref[b, 3]
        else:
            q_ref[a * n : a * n + n] = fine(query, before, NN)
            kv_ref[b * n : b * n + n, :width] = fine(key, after, NT)
            before, after = fine(x_ref[a, 3], before, NN), fine(after, x_ref[b, 3], NN)
    s_ref[...] = before


def near_kernel(x_ref, o_ref, m_ref, l_ref, key_ref, cat_ref, value_ref):
    blocks, _, n, width = x_ref.shape
    o_ref[:n] = jnp.zeros((n, width), F32)
    m_ref[:n] = jnp.full((n, 1), LOW, F32)
    l_ref[:n] = jnp.zeros((n, 1), F32)
    for a in range(1, blocks):
        last, rows = (a - 1) * n, a * n
        if a > 1:
            key_ref[:last] = mm(cat_ref[:last], left(x_ref[a - 1, 3], 1), NT)
        key_ref[last:rows] = x_ref[a - 1, 1]
        value_ref[last:rows] = x_ref[a - 1, 2].astype(BF16)
        cat_ref[:rows] = right(key_ref[:rows], 1)
        score = mm(left(x_ref[a, 0], 1), cat_ref[:rows], NT)
        top = jnp.max(score, -1, keepdims=True)
        weight = jnp.exp2(score - top)
        m_ref[rows : rows + n] = top
        l_ref[rows : rows + n] = jnp.sum(weight, -1, keepdims=True)
        o_ref[rows : rows + n] = mm(weight.astype(BF16), value_ref[:rows], NN)


def far_kernel(q_in, kv_hbm, maps_ref, o_in, m_in, l_in, out_ref, q_ref, o_ref, m_ref, l_ref, kv_ref, cat_ref, value_ref, sems):
    blocks, _, width = out_ref.shape
    n = width
    rows = q_in.shape[0]
    step = 256
    mine = lax.axis_index("sec")
    q_ref[...] = left(q_in[...], 1)
    o_ref[...] = o_in[...]
    m_ref[...] = m_in[...]
    l_ref[...] = l_in[...]

    def fetch(index):
        return pltpu.make_async_copy(kv_hbm.at[mine - 1 - index], kv_ref.at[index % 2], sems.at[index % 2])

    @pl.when(mine > 0)
    def _():
        fetch(0).start()

    def walk(index, carry):
        fetch(index).wait()

        @pl.when(index + 1 < mine)
        def _():
            fetch(index + 1).start()

        slot = index % 2
        cat_ref[...] = right(kv_ref[slot, :, :width], 1)
        value_ref[...] = kv_ref[slot, :, width:].astype(BF16)
        turn = right(maps_ref[mine - 1 - index], 0)

        def part(at, carry):
            here = pl.ds(pl.multiple_of(at * step, step), step)
            query = q_ref[here, :]
            score = mm(query, cat_ref[...], NT)
            old = m_ref[here, :]
            top = jnp.maximum(old, jnp.max(score, -1, keepdims=True))
            weight = jnp.exp2(score - top)
            factor = jnp.exp2(old - top)
            m_ref[here, :] = top
            l_ref[here, :] = l_ref[here, :] * factor + jnp.sum(weight, -1, keepdims=True)
            o_ref[here, :] = o_ref[here, :] * factor + mm(weight.astype(BF16), value_ref[...], NN)
            q_ref[here, :] = left(mm(query, turn, NN), 1)
            return carry

        return lax.fori_loop(0, rows // step, part, carry)

    lax.fori_loop(0, mine, walk, 0)
    row, col = grids(n)
    for a in range(blocks):
        here = slice(a * n, a * n + n)
        out_ref[a, :n] = o_ref[here]
        out_ref[a, n : n + 1] = as_row(m_ref[here], row == col)
        out_ref[a, n + 1 : n + 2] = as_row(l_ref[here], row == col)
        out_ref[a, n + 2 :] = jnp.zeros((WIDE - 2, width), F32)


def merge_kernel(far_ref, o_ref, m_ref, l_ref, out_ref):
    heads, n, width = o_ref.shape
    row, col = grids(n)
    for g in range(heads):
        far_top = as_column(far_ref[g, n : n + 1], row == col)
        far_sum = as_column(far_ref[g, n + 1 : n + 2], row == col)
        near_top = m_ref[g]
        top = jnp.maximum(far_top, near_top)
        far_factor, near_factor = jnp.exp2(far_top - top), jnp.exp2(near_top - top)
        total = far_sum * far_factor + l_ref[g] * near_factor
        mixed = far_ref[g, :n] * far_factor + o_ref[g] * near_factor
        out_ref[g] = (mixed / total).astype(BF16)


def shape(*dims, dtype=F32):
    return jax.ShapeDtypeStruct(dims, dtype)


def call(kernel, out_shape, *operands, scratch=(), in_specs=None, **params):
    return pl.pallas_call(
        kernel,
        out_shape=out_shape,
        in_specs=in_specs or [pl.BlockSpec(memory_space=pltpu.VMEM)] * len(operands),
        out_specs=jax.tree.map(lambda _: pl.BlockSpec(memory_space=pltpu.VMEM), out_shape),
        scratch_shapes=list(scratch),
        compiler_params=pltpu.CompilerParams(vmem_limit_bytes=VMEM_LIMIT, **params),
    )(*operands)


def body(query, key, value, raw_directions, beta_raw_logits):
    n, heads, width = query.shape
    kv_heads = key.shape[1]
    blocks = lax.axis_size("key")
    sections = lax.axis_size("sec")
    rows = n * blocks
    scale = width ** (-0.5) * math.log2(math.e)
    q, k, v, w = (jnp.transpose(x, (1, 0, 2)) for x in (query, key, value, raw_directions))
    sent, z, qw = call(
        functools.partial(terms_kernel, scale),
        [shape(heads, 4, n, width), shape(kv_heads, n, n), shape(heads, n, n)],
        q, k, v, w, beta_raw_logits,
    )
    near = lax.all_to_all(sent, "key", split_axis=0, concat_axis=0, tiled=True)
    own = call(
        functools.partial(diagonal_kernel, scale),
        [shape(heads, n, width), shape(heads, n, 1), shape(heads, n, 1)],
        q, k, v, z, qw,
    )
    section_query, section_kv, section_map = call(
        frames_kernel, [shape(rows, width), shape(rows, 2 * width), shape(width, width)], near
    )
    all_kv = lax.all_gather(section_kv, "sec")
    all_maps = lax.all_gather(section_map, "sec")
    state = call(
        near_kernel,
        [shape(rows, width), shape(rows, 1), shape(rows, 1)],
        near,
        scratch=[pltpu.VMEM((rows, width), F32), pltpu.VMEM((rows, 4 * width), BF16), pltpu.VMEM((rows, width), BF16)],
    )
    vmem = pl.BlockSpec(memory_space=pltpu.VMEM)
    back = call(
        far_kernel,
        shape(blocks, n + WIDE, width),
        section_query, all_kv, all_maps, *state,
        in_specs=[vmem, pl.BlockSpec(memory_space=pl.ANY)] + [vmem] * 4,
        scratch=[
            pltpu.VMEM((rows, 4 * width), BF16),
            pltpu.VMEM((rows, width), F32),
            pltpu.VMEM((rows, 1), F32),
            pltpu.VMEM((rows, 1), F32),
            pltpu.VMEM((2, rows, 2 * width), F32),
            pltpu.VMEM((rows, 4 * width), BF16),
            pltpu.VMEM((rows, width), BF16),
            pltpu.SemaphoreType.DMA((2,)),
        ],
    )
    far = lax.all_to_all(back, "key", split_axis=0, concat_axis=0, tiled=True)
    merged = call(merge_kernel, shape(heads, n, width, dtype=BF16), far, *own)
    return jnp.transpose(merged, (1, 0, 2))


def solution(mesh):
    spec = P(("sec", "key"), None, None)
    return jax.shard_map(
        body,
        mesh=mesh,
        in_specs=(spec, spec, spec, spec, P(("sec", "key"), None)),
        out_specs=spec,
        check_vma=False,
    )
```

time: 1170 us -> 305 us (0.26)
  the two profiles are of different devices: /device:TPU:26 before, /device:TPU:7 now
where the time goes in v1:
time: 305 us; the launch traced here: 304 us
  Pallas kernels  147 us (48%)
  blocking collectives  74.6 us (24%)
  waiting for transfers between devices  52.2 us (17%)
  between operations  13.4 us (4%)
  local copies, waits for them, and re-layouts  9.82 us (3%)
  starting transfers between devices  6.95 us (2%)
    pallas_call x6, Pallas kernels, call(): pl.pallas_call(kernel, out_shape=out_shape, in_specs=in_specs or [pl.Bloc...  147 us
    all_to_all x1, blocking collectives, body(): near = lax.all_to_all(sent, 'key', split_axis=0, concat_axis=0, tiled=True)  57.1 us
    all_gather x1, waiting for transfers between devices, body(): all_kv = lax.all_gather(section_kv, 'sec')  47.2 us
    all_gather x1, blocking collectives, body(): all_maps = lax.all_gather(section_map, 'sec')  17.5 us
    all_to_all x1, starting transfers between devices, body(): far = lax.all_to_all(back, 'key', split_axis=0, concat_axis=0, tiled=True)  6.95 us
  transfers between devices with their start and end apart: 2, of which 2 were waited for; matrix products, arithmetic and copies ran while one was open for 0% of the time, Pallas kernels for 9%

profile of v1, /device:TPU:7, one launch (start us, length us, event | category | flops | bytes accessed | tf_op | source)
XLA Modules:
  0.0 304.2 jit_solution(12171385025349030280)
XLA Ops:
  6.5 0.0 all-gather.4.cloned.1.call-start
  6.5 1.4 copy.10.b_ref
  7.9 1.6 copy.17
  9.5 2.0 copy.16
  11.5 1.7 copy_bitcast_fusion.1
  13.2 10.4 %shard_map.55 = (f32[16,4,128,128]{3,2,1,0:T(8,128)}, f32[4,128,128]{2,1,0:T(8,128)}, f32[16,128,128]{2,1,0:T(8,128)}) custom-call(bf16[16,128,128]{2,1,0:T(8,128)(2,1)} %bitcast.14, bf16[4,128,128]{2,1,0:T(8,128)(2,1)} %bitcast.18, bf16[4,128,128]{2,1,0:T(8,128)(2,1)} %get-tuple-element.30.v_ref, bf16[4,128,128]{2,1,0:T(8,128)(2,1)} %get-tuple-element.29.w_ref, ...), custom_call_target="tpu_custom_call" | custom-call | tf_op jit(solution)/shard_map/pallas_call | solution.py:229
  23.6 57.1 %all_to_all.10.x_ref = f32[16,4,128,128]{3,2,1,0:T(8,128)} all-to-all(f32[16,4,128,128]{3,2,1,0:T(8,128)} %get-tuple-element.17), channel_id=1, replica_groups=mesh['sec'=8,'key'=16] {'key'}, dimensions={0} | all-to-all | bytes 8388608 | tf_op jit(solution)/shard_map/all_to_all | solution.py:252
  80.7 7.5 %shard_map.56 = (f32[2048,128]{1,0:T(8,128)}, f32[2048,256]{1,0:T(8,128)}, f32[128,128]{1,0:T(8,128)}) custom-call(f32[16,4,128,128]{3,2,1,0:T(8,128)} %all_to_all.10.x_ref), custom_call_target="tpu_custom_call" | custom-call | tf_op jit(solution)/shard_map/pallas_call | solution.py:229
  88.2 0.0 copy-start.1
  88.2 0.0 all-gather.4.cloned.1.call-update
  88.2 21.6 %shard_map.57 = (f32[2048,128]{1,0:T(8,128)}, f32[2048,1]{1,0:T(8,128)}, f32[2048,1]{1,0:T(8,128)}) custom-call(f32[16,4,128,128]{3,2,1,0:T(8,128)} %all_to_all.10.x_ref), custom_call_target="tpu_custom_call" | custom-call | tf_op jit(solution)/shard_map/pallas_call | solution.py:229
  109.9 0.0 copy-done.1
  109.9 17.5 %all-gather.1 = f32[1024,128]{1,0:T(8,128)} all-gather(f32[128,128]{1,0:T(8,128)S(1)} %copy-done.1), channel_id=3, replica_groups=mesh['sec'=8,'key'=16] {'sec'}, dimensions={0}, use_global_device_ids=true | all-gather | bytes 589824 | tf_op jit(solution)/shard_map/all_gather | solution.py:262
  127.4 47.2 %all-gather.4.cloned.1.call-done = f32[16384,256]{1,0:T(8,128)} async-done(((f32[2048,256]{1,0:T(8,128)}), f32[16384,256]{1,0:T(8,128)}) %all-gather.4.cloned.1.call-update) | async-done | bytes 16777232 | tf_op jit(solution)/shard_map/all_gather | solution.py:261
  174.5 96.1 %shard_map.58 = f32[16,136,128]{2,1,0:T(8,128)} custom-call(f32[2048,128]{1,0:T(8,128)} %get-tuple-element.18.q_in, f32[8,2048,256]{2,1,0:T(8,128)} %bitcast.13, f32[8,128,128]{2,1,0:T(8,128)} %bitcast.16, f32[2048,128]{1,0:T(8,128)} %get-tuple-element.21.o_in, f32[2048,1]{1,0:T(8,128)} %get-tuple-element.22.m_in, f32[2048,1]{1,0:T(8,128)} %get-tuple-element.23.l_in), custom_call_target="tpu_custom_call" | custom-call | tf_op jit(solution)/shard_map/pallas_call | solution.py:229
  270.6 7.0 %all-to-all-start.1 = ((f32[16,136,128]{2,1,0:T(8,128)}), f32[16,136,128]{2,1,0:T(8,128)S(1)}, u32[]{:S(2)}, u32[]{:S(2)}) async-start(f32[16,136,128]{2,1,0:T(8,128)} %shard_map.58), calls=%async_computation.1 | async-start | bytes 2228224 | tf_op jit(solution)/shard_map/all_to_all | solution.py:286
  277.6 7.1 %shard_map.59 = (f32[16,128,128]{2,1,0:T(8,128)}, f32[16,128,1]{2,1,0:T(8,128)}, f32[16,128,1]{2,1,0:T(8,128)}) custom-call(bf16[16,128,128]{2,1,0:T(8,128)(2,1)} %bitcast.15, bf16[4,128,128]{2,1,0:T(8,128)(2,1)} %bitcast.19, bf16[4,128,128]{2,1,0:T(8,128)(2,1)} %get-tuple-element.30.v_ref, f32[4,128,128]{2,1,0:T(8,128)} %get-tuple-element.24.z_ref, ...), custom_call_target="tpu_custom_call" | custom-call | tf_op jit(solution)/shard_map/pallas_call | solution.py:229
  284.7 5.0 %all-to-all-done.1.far_ref = f32[16,136,128]{2,1,0:T(8,128)S(1)} async-done(((f32[16,136,128]{2,1,0:T(8,128)}), f32[16,136,128]{2,1,0:T(8,128)S(1)}, u32[]{:S(2)}, u32[]{:S(2)}) %all-to-all-start.1) | async-done | bytes 1114144 | tf_op jit(solution)/shard_map/all_to_all | solution.py:286
  289.7 0.0 copy-start
  289.7 1.0 copy-done
  290.7 4.5 %shard_map.60 = bf16[16,128,128]{2,1,0:T(8,128)(2,1)} custom-call(f32[16,136,128]{2,1,0:T(8,128)} %copy-done, f32[16,128,128]{2,1,0:T(8,128)} %get-tuple-element.26.o_ref, f32[16,128,1]{2,1,0:T(8,128)} %get-tuple-element.27.m_ref, f32[16,128,1]{2,1,0:T(8,128)} %get-tuple-element.28.l_ref), custom_call_target="tpu_custom_call" | custom-call | tf_op jit(solution)/shard_map/pallas_call | solution.py:229
  295.2 2.2 copy.11
Async XLA Ops:
  6.5 168.0 %all-gather.4.cloned.1.call-start = ((), (), s32[]{:S(2)}) async-start(), calls=%async_computation.2 | async-start | bytes 18874368 | tf_op jit(solution)/shard_map/all_gather | solution.py:261
  88.2 21.7 %copy-start.1 = (f32[128,128]{1,0:T(8,128)S(1)}, f32[128,128]{1,0:T(8,128)}, u32[]{:S(2)}) copy-start(f32[128,128]{1,0:T(8,128)} %get-tuple-element.20) | copy-start | bytes 196612
  270.6 19.1 %all-to-all-start.1 = ((f32[16,136,128]{2,1,0:T(8,128)}), f32[16,136,128]{2,1,0:T(8,128)S(1)}, u32[]{:S(2)}, u32[]{:S(2)}) async-start(f32[16,136,128]{2,1,0:T(8,128)} %shard_map.58), calls=%async_computation.1 | async-start | bytes 2228224 | tf_op jit(solution)/shard_map/all_to_all | solution.py:286
  289.7 1.0 copy-start
Sparse Core Ops, SparseCore 0:
  88.4 86.1 all-gather.3
